TPU v7x, 512 devices: a whole 4x4x16 slice. The times are simulated.
512 devices in a mesh: row: 128 (over z, y, core), col: 4 (over x).
Axes of the slice: x: 4, y: 4, z: 16, core: 2. Of those that a mesh axis runs over, the one named last changes fastest.
Arguments:
- left_values: bfloat16 [3, 131072, 512], P(None, 'row', 'col'), may hold values from -40 to 40
- left_pattern: int32 [3, 1024, 4], P(None, 'row', 'col'), may hold values from 0 to 1, as said below
- right_values: bfloat16 [131072, 2048], P('row', 'col'), may hold values from -0.25 to 0.25
- right_pattern: int32 [1024, 16], P('row', 'col'), may hold values from 0 to 1, as said below
Outputs:
- normalized: float32 [131072, 2048], P('row', 'col')
Inputs may be any that keep to these rules, and one draw needn't show every extreme that they name: `left_pattern`: in each panel, the 8 tiles of one device (aligned blocks of 8 tile rows, one tile column) hold 1 to 6 occupied tiles; in every panel some block of 8 tile rows holds 6 in each of its 4 tile columns. `right_pattern`: in every aligned block of 8 tile rows, each tile column has at least one occupied tile among the block's first 4 tile rows.
All inputs are finite; a program needn't handle non-finite values.
Results may differ from a plain program's by a relative error of at most 0.0003.
Values may be sent and summed in bfloat16 or wider, within the bound.
A program may use at most 64 MiB of HBM per device.

v0:
```python
import jax
import jax.numpy as jnp
from jax import lax
from jax.sharding import PartitionSpec as P

TILE = 128


def broadcast(x, axis, root):
    mine = lax.axis_index(axis) == root
    return lax.psum(jnp.where(mine, x, jnp.zeros_like(x)), axis)


def gather_left(masked):
    sections = masked.shape[0]
    tile_rows = masked.shape[1]
    flat = masked.reshape(sections, tile_rows * TILE, TILE)
    panel = lax.all_gather(flat, "col", axis=2, tiled=True)
    return panel


def on_device(left_values, left_pattern, right_values, right_pattern):
    sections = left_values.shape[0]
    tile_rows = left_pattern.shape[1]
    inner_tiles = lax.axis_size("col")
    span = inner_tiles * TILE
    tile_mask = jnp.repeat(jnp.repeat(right_pattern[:inner_tiles], TILE, axis=0), TILE, axis=1)
    own_panel = right_values[:span] * tile_mask.astype(jnp.bfloat16)
    root_step = lax.axis_size("row") // sections
    masked = left_values.reshape(sections, tile_rows, TILE, TILE) * left_pattern[
        :, :, :, None
    ].astype(jnp.bfloat16)
    total = jnp.zeros((tile_rows * TILE, right_values.shape[1]), jnp.float32)
    for section in range(sections):
        panel = gather_left(masked[section : section + 1])
        panel_right = broadcast(own_panel, "row", section * root_step)
        total = total + jnp.dot(panel[0], panel_right, preferred_element_type=jnp.float32)
    inflated = total * total
    column_total = lax.psum(jnp.sum(inflated, axis=0), "row")
    rows_total = tile_rows * TILE * lax.axis_size("row")
    return inflated * (rows_total / column_total)[None, :]


def solution(mesh):
    in_specs = (P(None, "row", "col"), P(None, "row", "col"), P("row", "col"), P("row", "col"))
    out_specs = P("row", "col")
    return jax.shard_map(
        on_device, mesh=mesh, in_specs=in_specs, out_specs=out_specs, check_vma=False
    )
```

profile of v0, /device:TPU:1, one launch (start us, length us, event | category | flops | bytes accessed | tf_op | source)
XLA Modules:
  0.0 631.5 jit_solution(13641505156577160336)
XLA Ops:
  7.4 0.0 all-reduce.3.cloned.1.call-start
  7.4 0.7 convert.3
  8.1 0.1 copy.5
  8.2 0.6 broadcast_in_dim.9
  8.8 0.0 copy-start.3
  8.8 0.0 copy-start
  8.8 2.4 broadcast_select_fusion
  11.2 0.0 all-reduce.3.cloned.1.call-update
  11.3 0.0 all-gather.6.cloned.1.call-start
  11.3 0.0 copy-done.3
  11.3 0.0 copy-done
  11.3 0.1 broadcast_multiply_fusion.1
  11.5 0.9 fusion.5
  12.4 0.0 all-gather.6.cloned.1.call-update
  12.4 0.0 all-gather.4.cloned.1.call-start
  12.5 0.5 all-gather.4.cloned.1.call-update
  13.0 0.0 all-gather.8.cloned.1.call-start
  13.1 0.5 all-gather.8.cloned.1.call-update
  13.6 348.5 %all-reduce.3.cloned.1.call-done = (bf16[512,512]{1,0:T(8,128)(2,1)}, bf16[512,512]{1,0:T(8,128)(2,1)}, bf16[512,512]{1,0:T(8,128)(2,1)}) async-done(((bf16[512,512]{1,0:T(8,128)(2,1)}, bf16[512,512]{1,0:T(8,128)(2,1)}, bf16[512,512]{1,0:T(8,128)(2,1)}), (bf16[512,512]{1,0:T(8,128)(2,1)}, bf16[512,512]{1,0:T(8,128)(2,1)}, bf16[512,512]{1,0:T(8,128)(2,1)})) %all-reduce.3.cloned.1.call-update) | async-done | bytes 1572880 | tf_op jit(solution)/shard_map/psum | solution.py:11
  362.1 0.0 copy-start.2
  362.1 0.0 all-gather.6.cloned.1.call-done
  362.1 2.1 fusion.1
  364.2 0.0 copy-start.1
  364.2 0.0 all-gather.4.cloned.1.call-done
  364.3 0.0 copy-done.2
  364.3 3.3 fusion.3
  367.6 0.0 all-gather.8.cloned.1.call-done
  367.6 0.0 copy-done.1
  367.6 4.0 fusion.6
  371.5 249.2 %psum.31 = f32[512]{0:T(512)S(1)} all-reduce(f32[512]{0:T(512)S(1)} %get-tuple-element.14), channel_id=1, replica_groups=mesh['row'=128,'col'=4] {'row'}, use_global_device_ids=true, to_apply=%region_4.5 | all-reduce | flops 512 | bytes 4096 | tf_op jit(solution)/shard_map/psum | solution.py:39
  620.8 3.2 broadcast_multiply_fusion
  (4 shorter events, 0.0 us)
Async XLA Ops:
  7.4 354.7 %all-reduce.3.cloned.1.call-start = ((), (), s32[]{:S(2)}) async-start(), calls=%async_computation.3 | async-start | bytes 3145728 | tf_op jit(solution)/shard_map/psum | solution.py:11
  8.8 2.5 copy-start.3
  8.8 2.5 copy-start
  11.3 350.8 %all-gather.6.cloned.1.call-start = ((), (), s32[]{:S(2)}) async-start(), calls=%async_computation.1 | async-start | bytes 1310720 | tf_op jit(solution)/shard_map/all_gather | solution.py:18
  12.4 351.8 %all-gather.4.cloned.1.call-start = ((), (), s32[]{:S(2)}) async-start(), calls=%async_computation | async-start | bytes 1310720 | tf_op jit(solution)/shard_map/all_gather | solution.py:18
  13.0 354.6 %all-gather.8.cloned.1.call-start = ((), (), s32[]{:S(2)}) async-start(), calls=%async_computation.2 | async-start | bytes 1310720 | tf_op jit(solution)/shard_map/all_gather | solution.py:18
  362.1 2.2 copy-start.2
  364.2 3.4 copy-start.1
Sparse Core Ops, SparseCore 0:
  11.8 350.2 all-reduce.2
Sparse Core Ops, SparseCore 1:
  14.0 37.4 all-gather.5
  53.7 34.0 all-gather.3
  89.9 34.1 all-gather.7
where the time goes:
time: 632 us
  waiting for transfers between devices  350 us (55%)
  blocking collectives  249 us (39%)
  between operations  15.1 us (2%)
  matrix products  9.37 us (1%)
  other arithmetic  6.38 us (1%)
    psum x1, waiting for transfers between devices, broadcast(): return lax.psum(jnp.where(mine, x, jnp.zeros_like(x)), axis)  349 us
    psum x1, blocking collectives, on_device(): column_total = lax.psum(jnp.sum(inflated, axis=0), 'row')  249 us
  transfers between devices with their start and end apart: 4, of which 1 were waited for; matrix products, arithmetic and copies ran while one was open for 1% of the time, Pallas kernels for 0%

commit v1 on v0

v1 whole, which is shorter than its diff:
```python
import jax
import jax.numpy as jnp
from jax import lax
from jax.experimental import pallas as pl
from jax.experimental.pallas import tpu as pltpu
from jax.sharding import PartitionSpec as P

TILE = 128
TR = 8
SLOTS = 6
HALF = SLOTS // 2
S = 3
NX, NZ, NG = 4, 16, 8
NY = 4
STEP = 42
COLS = 512
PIECE = 64
FIRST = S * 3 * TILE
MESH = pl.DeviceIdType.MESH
ORDER = (0, 1, 3, 2)


def base(s, q):
    return s * 3 * TILE + q * TILE if q < 3 else FIRST + s * TILE


def free_slots(pattern):
    first, last = SLOTS - 1, 0
    for i in range(SLOTS):
        last = jnp.where(pattern[i] == 0, i, last)
        first = jnp.where(pattern[SLOTS - 1 - i] == 0, SLOTS - 1 - i, first)
    return first, last


def kernel(left_hbm, pat, right_hbm, rpat, out, scale, own, pack, from_next, from_prev, from_far, pats, raw, root,
           left, right, mine, group, part, column, psend, precv, xsend, xrecv, rootsend, ownrecv, treesend, ysend, yrecv,
           csend, crecv, gsend, grecv, zsend, zrecv, load):
    r, x = lax.axis_index("row"), lax.axis_index("col")
    z, g = r // NG, r % NG
    y, c = g // 2, g % 2

    def at_x(d):
        return (r, (x + d) % NX)

    def at_z(d):
        return (((z + d) % NZ) * NG + g, x)

    def at_y(d):
        return (z * NG + ((y + d) % NY) * 2 + c, x)

    def at_g(d):
        return (z * NG + (g + d) % NG, x)

    sibling = (z * NG + y * 2 + 1 - c, x)

    def copy(src, dst, send, recv, to):
        return pltpu.make_async_remote_copy(src_ref=src, dst_ref=dst, send_sem=send, recv_sem=recv, device_id=to, device_id_type=MESH)

    barrier = pltpu.get_barrier_semaphore()
    peers = [at_x(d) for d in range(1, NX)] + [at_g(d) for d in range(1, NG)] + [at_z(d) for d in range(1, NZ)]
    for peer in peers:
        pl.semaphore_signal(barrier, inc=1, device_id=peer, device_id_type=MESH)

    loads = [pltpu.make_async_copy(left_hbm.at[s], own[s], load.at[s]) for s in range(S)]
    for cp in loads:
        cp.start()
    is_root = jnp.logical_and(r % STEP == 0, r // STEP < S)
    load_right = pltpu.make_async_copy(right_hbm.at[pl.ds(0, NX * TILE)], raw, load.at[S])

    def piece(s, p):
        return s * 3 * TILE + p * PIECE + (p // 6) * (FIRST + s * TILE - 6 * PIECE - s * 3 * TILE)

    def piece_of(s, p):
        return right.at[pl.ds(pl.multiple_of(piece(s, p), PIECE), PIECE)]

    @pl.when(is_root)
    def _():
        load_right.start()
        load_right.wait()
        for q, d in enumerate(ORDER):
            k = (x + d) % NX
            for j in range(COLS // TILE):
                tile = raw[pl.ds(pl.multiple_of(k * TILE, TILE), TILE), pl.ds(j * TILE, TILE)]
                root[pl.ds(q * TILE, TILE), pl.ds(j * TILE, TILE)] = jnp.where(rpat[k, j] != 0, tile, jnp.zeros_like(tile))

    own_pattern = [[pat[s, i] for i in range(TR)] for s in range(S)]
    for s in range(S):
        first, last = free_slots(own_pattern[s])
        loads[s].wait()
        for t in range(SLOTS):
            at = jnp.where(jnp.logical_and(own_pattern[s][TR - 2] != 0, first == t), TR - 2, t)
            at = jnp.where(jnp.logical_and(own_pattern[s][TR - 1] != 0, last == t), TR - 1, at)
            pack[s, t] = own[s][at]

    pl.semaphore_wait(barrier, len(peers))

    my_panel = r // STEP
    root_copies = [
        copy(root.at[pl.ds(pl.multiple_of(((g + d) % NG) * PIECE, PIECE), PIECE)], piece_of(my_panel, (g + d) % NG),
             rootsend.at[d - 1], ownrecv.at[my_panel], at_g(d))
        for d in range(1, NG)
    ]

    @pl.when(is_root)
    def _():
        for cp in root_copies:
            cp.start()
        start = pl.multiple_of(piece(my_panel, g), PIECE)
        right[pl.ds(start, PIECE)] = root[pl.ds(pl.multiple_of(g * PIECE, PIECE), PIECE)]

    pattern_copies = [copy(pat, pats[d], psend.at[d], precv.at[d], at_x(NX - d)) for d in range(1, NX)]
    for cp in pattern_copies:
        cp.start()
    halves = [pl.ds(0, HALF), pl.ds(HALF, HALF)]
    to_next = [[copy(pack.at[s, halves[h]], from_prev[s].at[halves[h]], xsend.at[0, s, h], xrecv.at[0, s, h], at_x(1)) for h in range(2)] for s in range(S)]
    to_prev = [[copy(pack.at[s, halves[h]], from_next[s].at[halves[h]], xsend.at[1, s, h], xrecv.at[1, s, h], at_x(NX - 1)) for h in range(2)] for s in range(S)]
    for h in range(2):
        for s in range(S):
            to_next[s][h].start()
            to_prev[s][1 - h].start()
    far_next = [copy(from_prev[s].at[halves[0]], from_far[s].at[halves[0]], xsend.at[2, s, 0], xrecv.at[2, s, 0], at_x(1)) for s in range(S)]
    far_prev = [copy(from_next[s].at[halves[1]], from_far[s].at[halves[1]], xsend.at[2, s, 1], xrecv.at[2, s, 1], at_x(NX - 1)) for s in range(S)]

    own_copies = [copy(piece_of(s, g), piece_of(s, g), rootsend.at[0], ownrecv.at[s], at_g(1)) for s in range(S)]
    far = 2 - c * 4 + NZ
    zero = [STEP * s // NG for s in range(S)]
    for s in range(S):
        hub_copies = [copy(piece_of(s, g), piece_of(s, g), treesend.at[i], ownrecv.at[s], at_z(d)) for i, d in enumerate((8, 4, 12))]

        @pl.when(z == zero[s])
        def _():
            @pl.when(g != STEP * s % NG)
            def _():
                own_copies[s].wait_recv()

            for cp in hub_copies:
                cp.start()

    for s in range(S):
        rel = (z - zero[s] + NZ) % NZ
        leaf_copies = [copy(piece_of(s, g), piece_of(s, g), treesend.at[3 + i], ownrecv.at[s], at_z(d)) for i, d in enumerate((far, 1, NZ - 1))]

        @pl.when(rel % 4 == 0)
        def _():
            @pl.when(rel != 0)
            def _():
                own_copies[s].wait_recv()

            for cp in leaf_copies:
                cp.start()

    y_copies, c_copies = [], []
    for s in range(S):
        rel = (z - zero[s] + NZ) % NZ

        @pl.when(rel % 4 != 0)
        def _():
            own_copies[s].wait_recv()

        y_copies.append([copy(piece_of(s, g), piece_of(s, g), ysend.at[s, d - 1], yrecv.at[s, d - 1], at_y(d)) for d in range(1, NY)])
        c_copies.append([copy(piece_of(s, (g + NG - 2 * d) % NG), piece_of(s, (g + NG - 2 * d) % NG), csend.at[s, d], crecv.at[s, d], sibling) for d in range(NY)])
        for d in (2, 1, 3):
            y_copies[s][d - 1].start()
        c_copies[s][0].start()

    def place(s, q, pattern, tiles, low, high):
        for i, tile in zip((0, 1, 2, 3, 4, 5, 6, 7), (0, 1, 2, 3, 4, 5, low, high)):
            value = tiles[tile]
            left[pl.ds(i * TILE, TILE), pl.ds(base(s, q), TILE)] = jnp.where(pattern[i] != 0, value, jnp.zeros_like(value))

    for s in range(S):
        place(s, 0, own_pattern[s], own[s], TR - 2, TR - 1)

    for s in range(S):
        to_next[s][0].wait_recv()
        far_next[s].start()
        to_prev[s][1].wait_recv()
        far_prev[s].start()

    for s in range(S):
        for d in (1, 3, 2):
            y_copies[s][d - 1].wait_recv()
            c_copies[s][d].start()

    for cp in pattern_copies:
        cp.wait_recv()

    def received(s, q, tiles):
        pattern = [pats[ORDER[q]][s, i] for i in range(TR)]
        first, last = free_slots(pattern)
        place(s, q, pattern, tiles, first, last)

    for s in range(S):
        to_next[s][1].wait_recv()
        to_prev[s][0].wait_recv()
        received(s, 1, from_next[s])
        received(s, 2, from_prev[s])

    for s in range(S):
        for d in range(NY):
            c_copies[s][d].wait_recv()

    for n in range(2):
        cols = pl.ds(n * 256, 256)
        out[:, cols] = jnp.dot(left[:, :FIRST], right[:FIRST, cols], preferred_element_type=jnp.float32)

    for s in range(S):
        far_next[s].wait_recv()
        far_prev[s].wait_recv()
        received(s, 3, from_far[s])

    for n in range(2):
        cols = pl.ds(n * 256, 256)
        total = out[:, cols] + jnp.dot(left[:, FIRST:], right[FIRST:, cols], preferred_element_type=jnp.float32)
        total = total * total
        out[:, cols] = total
        mine[:, cols] = jnp.sum(total, axis=0, keepdims=True)

    g_copies = [copy(mine, group.at[d - 1], gsend.at[d - 1], grecv.at[d - 1], at_g(d)) for d in range(1, NG)]
    for cp in g_copies:
        cp.start()
    for cp in g_copies:
        cp.wait_recv()
    part[...] = mine[...] + jnp.sum(group[...], axis=0)
    z_copies = [copy(part, column.at[d - 1], zsend.at[d - 1], zrecv.at[d - 1], at_z(d)) for d in range(1, NZ)]
    for cp in z_copies:
        cp.start()
    for cp in z_copies:
        cp.wait_recv()
    rows_total = TR * TILE * NZ * NG
    scale[...] = rows_total / (part[...] + jnp.sum(column[...], axis=0))

    @pl.when(is_root)
    def _():
        for cp in root_copies:
            cp.wait_send()

    for s in range(S):
        waiter = [copy(piece_of(s, g), piece_of(s, g), treesend.at[i], ownrecv.at[s], at_z(1)) for i in range(6)]

        @pl.when(z == zero[s])
        def _():
            for cp in waiter[:3]:
                cp.wait_send()

        @pl.when((z - zero[s] + NZ) % NZ % 4 == 0)
        def _():
            for cp in waiter[3:]:
                cp.wait_send()

    flat = pattern_copies + far_next + far_prev + g_copies + z_copies
    for group_of in to_next + to_prev + y_copies + c_copies:
        flat = flat + group_of
    for cp in flat:
        cp.wait_send()


def on_device(left_values, left_pattern, right_values, right_pattern):
    tiles = left_values.reshape(S, TR, TILE, TILE)
    pattern = left_pattern.reshape(S, TR)
    rows = TR * TILE
    dma = pltpu.SemaphoreType.DMA
    box = lambda n: tuple(pltpu.VMEM((n, TILE, TILE), jnp.bfloat16) for _ in range(S))
    any_space, smem, vmem = (pl.BlockSpec(memory_space=m) for m in (pl.ANY, pltpu.SMEM, pltpu.VMEM))
    squares, scale = pl.pallas_call(
        kernel,
        out_shape=(pltpu.VMEM((rows, COLS), jnp.float32), pltpu.VMEM((1, COLS), jnp.float32)),
        in_specs=[any_space, smem, any_space, smem],
        out_specs=(vmem, vmem),
        scratch_shapes=[
            box(TR),
            pltpu.VMEM((S, SLOTS, TILE, TILE), jnp.bfloat16),
            box(SLOTS), box(SLOTS), box(SLOTS),
            tuple(pltpu.SMEM((S, TR), jnp.int32) for _ in range(NX)),
            pltpu.VMEM((NX * TILE, COLS), jnp.bfloat16),
            pltpu.VMEM((NX * TILE, COLS), jnp.bfloat16),
            pltpu.VMEM((rows, S * NX * TILE), jnp.bfloat16),
            pltpu.VMEM((S * NX * TILE, COLS), jnp.bfloat16),
            pltpu.VMEM((1, COLS), jnp.float32),
            pltpu.VMEM((NG - 1, 1, COLS), jnp.float32),
            pltpu.VMEM((1, COLS), jnp.float32),
            pltpu.VMEM((NZ - 1, 1, COLS), jnp.float32),
            dma((NX,)), dma((NX,)),
            dma((3, S, 2)), dma((3, S, 2)),
            dma((NG - 1,)), dma((S,)), dma((6,)),
            dma((S, NY - 1)), dma((S, NY - 1)),
            dma((S, NY)), dma((S, NY)),
            dma((NG - 1,)), dma((NG - 1,)),
            dma((NZ - 1,)), dma((NZ - 1,)),
            dma((S + 1,)),
        ],
        compiler_params=pltpu.CompilerParams(collective_id=0, has_side_effects=True, vmem_limit_bytes=48 * 1024 * 1024),
    )(tiles, pattern, right_values, right_pattern)
    return squares * scale


def solution(mesh):
    in_specs = (P(None, "row", "col"), P(None, "row", "col"), P("row", "col"), P("row", "col"))
    out_specs = P("row", "col")
    return jax.shard_map(
        on_device, mesh=mesh, in_specs=in_specs, out_specs=out_specs, check_vma=False
    )
```

time: 632 us -> 65 us (0.10)
  waiting for transfers between devices: 350 us -> 0 us
  blocking collectives: 249 us -> 0 us
  Pallas kernels: 0 us -> 59.4 us
  between operations: 15.1 us -> 0.01 us
  matrix products: 9.37 us -> 0 us
    psum x1 -> x0, waiting for transfers between devices: 349 us -> none  [broadcast(): return lax.psum(jnp.where(mine, x, jnp.zeros_like(x)), axis)]
    psum x1 -> x0, blocking collectives: 249 us -> none  [on_device(): column_total = lax.psum(jnp.sum(inflated, axis=0), 'row')]
    pallas_call x0 -> x1, Pallas kernels: none -> 59.4 us  [on_device(): pl.pallas_call(kernel, out_shape=(pltpu.VMEM((rows, COLS), jnp.float32),...]
    dot_general x3 -> x0, matrix products: 9.37 us -> none  [on_device(): jnp.dot(panel[0], panel_right, preferred_element_type=jnp.float32)]
  transfers between devices with their start and end apart: 4 -> 0, of which waited for: 1 -> 0; matrix products, arithmetic and copies ran while one was open for 1% -> 0% of each run, Pallas kernels for 0% -> 0%
where the time goes in v1:
time: 65 us; the launch traced here: 64.7 us
  Pallas kernels  59.4 us (91%)
  local copies, waits for them, and re-layouts  3.79 us (6%)
  other arithmetic  1.56 us (2%)
    pallas_call x1, Pallas kernels, on_device(): pl.pallas_call(kernel, out_shape=(pltpu.VMEM((rows, COLS), jnp.float32),...  59.4 us
    unnamed x6, local copies, waits for them, and re-layouts  3.79 us
    mul x1, other arithmetic, on_device(): return squares * scale  1.56 us

profile of v1, /device:TPU:1, one launch (start us, length us, event | category | flops | bytes accessed | tf_op | source)
XLA Modules:
  0.0 64.7 jit_solution(15722351479019103254)
XLA Ops:
  0.0 0.7 %copy.8 = s32[3,8,1]{1,0,2:T(4,128)S(1)} copy(s32[3,8,1]{1,2,0:T(1,128)} %param.5) | data formatting | bytes 192
  0.7 0.8 %copy.5.rpat = s32[8,4]{1,0:T(8,128)S(1)} copy(s32[8,4]{0,1:T(4,128)} %param.7) | data formatting | bytes 256 | tf_op args[3]
  1.4 0.0 copy-start
  1.4 1.2 %copy-done = bf16[1024,512]{1,0:T(8,128)(2,1)S(1)} copy-done((bf16[1024,512]{1,0:T(8,128)(2,1)S(1)}, bf16[1024,512]{1,0:T(8,128)(2,1)}, u32[]{:S(2)}) %copy-start) | copy-done | bytes 1048600
  2.7 0.0 copy-start.1
  2.7 1.1 %copy-done.1 = bf16[3,1024,128]{2,1,0:T(8,128)(2,1)S(1)} copy-done((bf16[3,1024,128]{2,1,0:T(8,128)(2,1)S(1)}, bf16[3,1024,128]{2,1,0:T(8,128)(2,1)}, u32[]{:S(2)}) %copy-start.1) | copy-done | bytes 786456
  3.8 59.4 %shard_map.46 = (f32[1024,512]{1,0:T(8,128)S(1)}, f32[1,512]{1,0:T(1,128)S(1)}) custom-call(bf16[3,8,128,128]{3,2,1,0:T(8,128)(2,1)S(1)} %bitcast.5, s32[3,8]{1,0:T(4,128)S(1)} %bitcast.6, bf16[1024,512]{1,0:T(8,128)(2,1)S(1)} %copy-done, s32[8,4]{1,0:T(8,128)S(1)} %copy.5.rpat), custom_call_target="tpu_custom_call" | custom-call | tf_op jit(solution)/shard_map/pallas_call | solution.py:265
  63.2 1.6 %broadcast_multiply_fusion = f32[1024,512]{1,0:T(8,128)} fusion(f32[1024,512]{1,0:T(8,128)S(1)} %get-tuple-element.7, f32[512]{0:T(512)S(1)} %bitcast.7), kind=kLoop, calls=%fused_computation | loop fusion | flops 524288 | bytes 4196352 | tf_op jit(solution)/shard_map/mul | solution.py:294
Async XLA Ops:
  1.4 1.2 %copy-start = (bf16[1024,512]{1,0:T(8,128)(2,1)S(1)}, bf16[1024,512]{1,0:T(8,128)(2,1)}, u32[]{:S(2)}) copy-start(bf16[1024,512]{1,0:T(8,128)(2,1)} %right_hbm.1) | copy-start | bytes 3145732
  2.7 1.1 %copy-start.1 = (bf16[3,1024,128]{2,1,0:T(8,128)(2,1)S(1)}, bf16[3,1024,128]{2,1,0:T(8,128)(2,1)}, u32[]{:S(2)}) copy-start(bf16[3,1024,128]{2,1,0:T(8,128)(2,1)} %param.4) | copy-start | bytes 2359300

commit v2 on v1

v2 whole, which is shorter than its diff:
```python
import jax
import jax.numpy as jnp
from jax import lax
from jax.experimental import pallas as pl
from jax.experimental.pallas import tpu as pltpu
from jax.sharding import PartitionSpec as P

TILE = 128
TR = 8
SLOTS = 6
HALF = SLOTS // 2
S = 3
NX, NZ, NG = 4, 16, 8
NY = 4
STEP = 42
COLS = 512
PIECE = 64
FIRST = S * 3 * TILE
MESH = pl.DeviceIdType.MESH
ORDER = (0, 1, 3, 2)


def base(s, q):
    return s * 3 * TILE + q * TILE if q < 3 else FIRST + s * TILE


def free_slots(pattern):
    first, last = SLOTS - 1, 0
    for i in range(SLOTS):
        last = jnp.where(pattern[i] == 0, i, last)
        first = jnp.where(pattern[SLOTS - 1 - i] == 0, SLOTS - 1 - i, first)
    return first, last


def kernel(left_hbm, pat, right_hbm, rpat, out, scale, own, pack, from_next, from_prev, from_far, pats, raw, root, spare,
           left, right, mine, other, pair, chips, part, column, psend, precv, xsend, xrecv, rootsend, sparerecv, ownrecv, treesend,
           ysend, yrecv, csend, crecv, asend, arecv, zsend, zrecv, load, known):
    r, x = lax.axis_index("row"), lax.axis_index("col")
    z, g = r // NG, r % NG
    y, c = g // 2, g % 2

    def at_x(d):
        return (r, (x + d) % NX)

    def at_z(d):
        return (((z + d + NZ) % NZ) * NG + g, x)

    def at_y(d):
        return (z * NG + ((y + d) % NY) * 2 + c, x)

    sibling = (z * NG + y * 2 + 1 - c, x)

    def copy(src, dst, send, recv, to):
        return pltpu.make_async_remote_copy(src_ref=src, dst_ref=dst, send_sem=send, recv_sem=recv, device_id=to, device_id_type=MESH)

    barrier = pltpu.get_barrier_semaphore()
    peers = [at_x(d) for d in range(1, NX)] + [at_y(d) for d in range(1, NY)] + [sibling] + [at_z(d) for d in (1, NZ - 1)]
    for peer in peers:
        pl.semaphore_signal(barrier, inc=1, device_id=peer, device_id_type=MESH)

    loads = [pltpu.make_async_copy(left_hbm.at[s], own[s], load.at[s]) for s in range(S)]
    for cp in loads:
        cp.start()
    is_root = jnp.logical_and(r % STEP == 0, r // STEP < S)
    load_right = pltpu.make_async_copy(right_hbm.at[pl.ds(0, NX * TILE)], raw, load.at[S])

    def piece(s, p):
        return s * 3 * TILE + p * PIECE + (p // 6) * (FIRST + s * TILE - 6 * PIECE - s * 3 * TILE)

    def piece_of(s, p):
        return right.at[pl.ds(pl.multiple_of(piece(s, p), PIECE), PIECE)]

    @pl.when(is_root)
    def _():
        load_right.start()
        load_right.wait()
        for q, d in enumerate(ORDER):
            k = (x + d) % NX
            for j in range(COLS // TILE):
                tile = raw[pl.ds(pl.multiple_of(k * TILE, TILE), TILE), pl.ds(j * TILE, TILE)]
                root[pl.ds(q * TILE, TILE), pl.ds(j * TILE, TILE)] = jnp.where(rpat[j, k] != 0, tile, jnp.zeros_like(tile))

    own_pattern = [[pat[s, 0, i] for i in range(TR)] for s in range(S)]
    for s in range(S):
        first, last = free_slots(own_pattern[s])
        loads[s].wait()
        for t in range(SLOTS):
            at = jnp.where(jnp.logical_and(own_pattern[s][TR - 2] != 0, first == t), TR - 2, t)
            at = jnp.where(jnp.logical_and(own_pattern[s][TR - 1] != 0, last == t), TR - 1, at)
            pack[s, t] = own[s][at]

    pl.semaphore_wait(barrier, len(peers))

    def wider(step):
        for to in (1 << step, NZ - (1 << step)):
            pl.semaphore_signal(known.at[step], inc=1, device_id=at_z(to), device_id_type=MESH)

    wider(0)

    my_panel = r // STEP

    def of_root(p):
        return root.at[pl.ds(pl.multiple_of(p * PIECE, PIECE), PIECE)]

    root_copies = []
    for d in range(1, NY):
        p = (g + 2 * d) % NG
        root_copies.append(copy(of_root(p), piece_of(my_panel, p), rootsend.at[2 * d - 2], ownrecv.at[my_panel], at_y(d)))
        root_copies.append(copy(of_root((p + 1) % NG), spare, rootsend.at[2 * d - 1], sparerecv.at[0], at_y(d)))
    root_copies.append(copy(of_root(g + 1 - 2 * c), piece_of(my_panel, g + 1 - 2 * c), rootsend.at[6], ownrecv.at[my_panel], sibling))

    @pl.when(is_root)
    def _():
        for i in (3, 6, 1, 5, 2, 0, 4):
            root_copies[i].start()
        start = pl.multiple_of(piece(my_panel, g), PIECE)
        right[pl.ds(start, PIECE)] = root[pl.ds(pl.multiple_of(g * PIECE, PIECE), PIECE)]

    pattern_copies = [copy(pat, pats[d], psend.at[d], precv.at[d], at_x(NX - d)) for d in range(1, NX)]
    for cp in pattern_copies:
        cp.start()
    halves = [pl.ds(0, HALF), pl.ds(HALF, HALF)]
    to_next = [[copy(pack.at[s, halves[h]], from_prev[s].at[halves[h]], xsend.at[0, s, h], xrecv.at[0, s, h], at_x(1)) for h in range(2)] for s in range(S)]
    to_prev = [[copy(pack.at[s, halves[h]], from_next[s].at[halves[h]], xsend.at[1, s, h], xrecv.at[1, s, h], at_x(NX - 1)) for h in range(2)] for s in range(S)]
    for s, h in ((0, 0), (1, 0), (2, 0), (0, 1)):
        to_next[s][h].start()
        to_prev[s][1 - h].start()
    far_next = [copy(from_prev[s].at[halves[0]], from_far[s].at[halves[0]], xsend.at[2, s, 0], xrecv.at[2, s, 0], at_x(1)) for s in range(S)]
    far_prev = [copy(from_next[s].at[halves[1]], from_far[s].at[halves[1]], xsend.at[2, s, 1], xrecv.at[2, s, 1], at_x(NX - 1)) for s in range(S)]

    def along_z(s, send, d):
        return copy(piece_of(s, g), piece_of(s, g), send, ownrecv.at[s], at_z(d))

    zero = [STEP * s // NG for s in range(S)]
    for s in range(S):
        own_copy = along_z(s, treesend.at[0], 4)
        spare_copy = copy(spare, piece_of(s, g + 1 - 2 * c), rootsend.at[6], ownrecv.at[s], sibling)
        spare_wait = copy(spare, spare, rootsend.at[6], sparerecv.at[0], sibling)

        @pl.when(z == zero[s])
        def _():
            @pl.when(jnp.logical_and(g != STEP * s % NG, c == 0))
            def _():
                spare_wait.wait_recv()
                spare_copy.start()

            @pl.when(g != STEP * s % NG)
            def _():
                own_copy.wait_recv()

    for s in range(S):
        next_copies = [along_z(s, treesend.at[i], d) for i, d in enumerate((1, -1))]

        @pl.when(z == zero[s])
        def _():
            for cp in next_copies:
                cp.start()

    pl.semaphore_wait(known.at[0], 2)
    wider(1)
    pl.semaphore_wait(known.at[1], 2)
    wider(2)
    for s in range(S):
        hub_copies = [along_z(s, treesend.at[2 + i], d) for i, d in enumerate((4, -4, 2, -2))]

        @pl.when(z == zero[s])
        def _():
            for cp in hub_copies:
                cp.start()

    for s in range(S):
        to_next[s][0].wait_recv()
        far_next[s].start()
        to_prev[s][1].wait_recv()
        far_prev[s].start()
        if s + 1 < S:
            to_next[s + 1][1].start()
            to_prev[s + 1][0].start()

    def place(s, q, pattern, tiles, low, high):
        for i, tile in zip((0, 1, 2, 3, 4, 5, 6, 7), (0, 1, 2, 3, 4, 5, low, high)):
            value = tiles[tile]
            left[pl.ds(i * TILE, TILE), pl.ds(base(s, q), TILE)] = jnp.where(pattern[i] != 0, value, jnp.zeros_like(value))

    for s in range(S):
        place(s, 0, own_pattern[s], own[s], TR - 2, TR - 1)

    rels = [(z - zero[s] + NZ) % NZ for s in range(S)]
    near = [jnp.where(rel % 8 == 4, -1, jnp.minimum(rel, NZ - rel)) for rel in rels]
    closest = jnp.where(jnp.logical_and(near[0] <= near[1], near[0] <= near[2]), 0, jnp.where(near[1] <= near[2], 1, 2))
    farthest = jnp.where(jnp.logical_and(near[2] >= near[0], near[2] >= near[1]), 2, jnp.where(near[1] >= near[0], 1, 0))
    panels = (closest, 3 - closest - farthest, farthest)
    y_copies, c_copies = [], []
    for n, s in enumerate(panels):
        rel = (z - STEP * s // NG + NZ) % NZ
        way = 1 - rel // 8 * 2
        relay_copies = [along_z(s, treesend.at[i], way * d) for i, d in enumerate((4, 3, 2, 1, -1))]

        @pl.when(rel != 0)
        def _():
            along_z(s, treesend.at[0], 4).wait_recv()

        @pl.when(rel == 4 + 8 * c)
        def _():
            relay_copies[0].start()

        @pl.when(rel % 8 == 4)
        def _():
            for cp in relay_copies[1:]:
                cp.start()

        y_copies.append([copy(piece_of(s, g), piece_of(s, g), ysend.at[s, d - 1], yrecv.at[s, d - 1], at_y(d)) for d in range(1, NY)])
        c_copies.append([copy(piece_of(s, (g + NG - 2 * d) % NG), piece_of(s, (g + NG - 2 * d) % NG), csend.at[s, d], crecv.at[s, d], sibling) for d in range(NY)])
        for d in (2, 1, 3):
            y_copies[n][d - 1].start()
        c_copies[n][0].start()

    for cp in pattern_copies:
        cp.wait_recv()

    def received(s, q, tiles):
        pattern = [pats[ORDER[q]][s, 0, i] for i in range(TR)]
        first, last = free_slots(pattern)
        place(s, q, pattern, tiles, first, last)

    for s in range(S):
        to_next[s][1].wait_recv()
        to_prev[s][0].wait_recv()
        received(s, 1, from_next[s])
        received(s, 2, from_prev[s])

    pl.semaphore_wait(known.at[2], 2)

    for s in range(S):
        for d in (1, 3, 2):
            y_copies[s][d - 1].wait_recv()
            c_copies[s][d].start()

    for s in range(S):
        for d in range(NY):
            c_copies[s][d].wait_recv()

    for n in range(2):
        cols = pl.ds(n * 256, 256)
        out[:, cols] = jnp.dot(left[:, :FIRST], right[:FIRST, cols], preferred_element_type=jnp.float32)

    for s in range(S):
        far_next[s].wait_recv()
        far_prev[s].wait_recv()
        received(s, 3, from_far[s])

    for n in range(2):
        cols = pl.ds(n * 256, 256)
        total = out[:, cols] + jnp.dot(left[:, FIRST:], right[FIRST:, cols], preferred_element_type=jnp.float32)
        total = total * total
        out[:, cols] = total
        mine[:, cols] = jnp.sum(total, axis=0, keepdims=True)

    across = copy(mine, other, asend.at[0], arecv.at[0], sibling)
    across.start()
    across.wait_recv()
    pair[...] = mine[...] + other[...]
    a_copies = [copy(pair, chips.at[d - 1], asend.at[d], arecv.at[d], at_y(d)) for d in range(1, NY)]
    for cp in a_copies:
        cp.start()
    for cp in a_copies:
        cp.wait_recv()
    part[...] = pair[...] + jnp.sum(chips[...], axis=0)
    z_copies = [copy(part, column.at[d - 1], zsend.at[d - 1], zrecv.at[d - 1], at_z(d)) for d in range(1, NZ)]
    for d in sorted(range(1, NZ), key=lambda d: -min(d, NZ - d)):
        z_copies[d - 1].start()
    for cp in z_copies:
        cp.wait_recv()
    rows_total = TR * TILE * NZ * NG
    scale[...] = rows_total / (part[...] + jnp.sum(column[...], axis=0))

    @pl.when(is_root)
    def _():
        for cp in root_copies:
            cp.wait_send()

    for s in range(S):
        waiter = [along_z(s, treesend.at[i], 1) for i in range(6)]
        spare_copy = copy(spare, piece_of(s, g + 1 - 2 * c), rootsend.at[6], ownrecv.at[s], sibling)
        rel = rels[s]

        @pl.when(rel == 0)
        def _():
            for cp in waiter:
                cp.wait_send()

        @pl.when(jnp.logical_and(rel == 0, jnp.logical_and(g != STEP * s % NG, c == 0)))
        def _():
            spare_copy.wait_send()

        @pl.when(rel == 4 + 8 * c)
        def _():
            waiter[0].wait_send()

        @pl.when(rel % 8 == 4)
        def _():
            for cp in waiter[1:5]:
                cp.wait_send()

    flat = pattern_copies + far_next + far_prev + [across] + a_copies + z_copies
    for group_of in to_next + to_prev + y_copies + c_copies:
        flat = flat + group_of
    for cp in flat:
        cp.wait_send()


def on_device(left_values, left_pattern, right_values, right_pattern):
    tiles = left_values.reshape(S, TR, TILE, TILE)
    pattern = left_pattern.transpose(0, 2, 1)
    rows = TR * TILE
    dma = pltpu.SemaphoreType.DMA
    box = lambda n: tuple(pltpu.VMEM((n, TILE, TILE), jnp.bfloat16) for _ in range(S))
    any_space, smem, vmem = (pl.BlockSpec(memory_space=m) for m in (pltpu.HBM, pltpu.SMEM, pltpu.VMEM))
    squares, scale = pl.pallas_call(
        kernel,
        out_shape=(pltpu.VMEM((rows, COLS), jnp.float32), pltpu.VMEM((1, COLS), jnp.float32)),
        in_specs=[any_space, smem, any_space, smem],
        out_specs=(vmem, vmem),
        scratch_shapes=[
            box(TR),
            pltpu.VMEM((S, SLOTS, TILE, TILE), jnp.bfloat16),
            box(SLOTS), box(SLOTS), box(SLOTS),
            tuple(pltpu.SMEM((S, 1, TR), jnp.int32) for _ in range(NX)),
            pltpu.VMEM((NX * TILE, COLS), jnp.bfloat16),
            pltpu.VMEM((NX * TILE, COLS), jnp.bfloat16),
            pltpu.VMEM((PIECE, COLS), jnp.bfloat16),
            pltpu.VMEM((rows, S * NX * TILE), jnp.bfloat16),
            pltpu.VMEM((S * NX * TILE, COLS), jnp.bfloat16),
            pltpu.VMEM((1, COLS), jnp.float32),
            pltpu.VMEM((1, COLS), jnp.float32),
            pltpu.VMEM((1, COLS), jnp.float32),
            pltpu.VMEM((NY - 1, 1, COLS), jnp.float32),
            pltpu.VMEM((1, COLS), jnp.float32),
            pltpu.VMEM((NZ - 1, 1, COLS), jnp.float32),
            dma((NX,)), dma((NX,)),
            dma((3, S, 2)), dma((3, S, 2)),
            dma((NG - 1,)), dma((1,)), dma((S,)), dma((6,)),
            dma((S, NY - 1)), dma((S, NY - 1)),
            dma((S, NY)), dma((S, NY)),
            dma((NY,)), dma((NY,)),
            dma((NZ - 1,)), dma((NZ - 1,)),
            dma((S + 1,)),
            pltpu.SemaphoreType.REGULAR((3,)),
        ],
        compiler_params=pltpu.CompilerParams(collective_id=0, has_side_effects=True, vmem_limit_bytes=56 * 1024 * 1024),
    )(*[pltpu.with_memory_space_constraint(a, pltpu.HBM) for a in (tiles, pattern, right_values, right_pattern.T)])
    return squares * scale


def solution(mesh):
    in_specs = (P(None, "row", "col"), P(None, "row", "col"), P("row", "col"), P("row", "col"))
    out_specs = P("row", "col")
    return jax.shard_map(
        on_device, mesh=mesh, in_specs=in_specs, out_specs=out_specs, check_vma=False
    )
```

time: 65 us -> 54.4 us (0.84)
  the two profiles are of different devices: /device:TPU:1 before, /device:TPU:2 now
where the time goes in v2:
time: 54.4 us; the launch traced here: 54.2 us
  Pallas kernels  52.7 us (97%)
  other arithmetic  1.57 us (3%)
    pallas_call x1, Pallas kernels, on_device(): pl.pallas_call(kernel, out_shape=(pltpu.VMEM((rows, COLS), jnp.float32),...  52.7 us
    mul x1, other arithmetic, on_device(): return squares * scale  1.57 us

profile of v2, /device:TPU:2, one launch (start us, length us, event | category | flops | bytes accessed | tf_op | source)
XLA Modules:
  0.0 54.2 jit_solution(7639516553240929297)
XLA Ops:
  0.0 52.7 %shard_map.46 = (f32[1024,512]{1,0:T(8,128)S(1)}, f32[1,512]{1,0:T(1,128)S(1)}) custom-call(bf16[3,8,128,128]{3,2,1,0:T(8,128)(2,1)} %bitcast.5, s32[3,1,8]{2,1,0:T(1,128)} %bitcast.7, bf16[1024,512]{1,0:T(8,128)(2,1)} %right_hbm.1, s32[4,8]{1,0:T(4,128)} %bitcast.6), custom_call_target="tpu_custom_call" | custom-call | tf_op jit(solution)/shard_map/pallas_call | solution.py:319
  52.7 1.6 %broadcast_multiply_fusion = f32[1024,512]{1,0:T(8,128)} fusion(f32[1024,512]{1,0:T(8,128)S(1)} %get-tuple-element.7, f32[512]{0:T(512)S(1)} %bitcast.4), kind=kLoop, calls=%fused_computation | loop fusion | flops 524288 | bytes 4196352 | tf_op jit(solution)/shard_map/mul | solution.py:352

commit v3 on v2

v3 whole, which is shorter than its diff:
```python
import jax
import jax.numpy as jnp
from jax import lax
from jax.experimental import pallas as pl
from jax.experimental.pallas import tpu as pltpu
from jax.sharding import PartitionSpec as P

TILE = 128
TR = 8
SLOTS = 6
HALF = SLOTS // 2
S = 3
NX, NZ, NG = 4, 16, 8
NY = 4
STEP = 42
COLS = 512
PIECE = 64
PART = 32
PARTS = PIECE // PART
INNER = NX * TILE
MESH = pl.DeviceIdType.MESH
ORDER = (0, 1, 3, 2)


def base(s, q):
    return s * INNER + q * TILE


def free_slots(pattern):
    first, last = SLOTS - 1, 0
    for i in range(SLOTS):
        last = jnp.where(pattern[i] == 0, i, last)
        first = jnp.where(pattern[SLOTS - 1 - i] == 0, SLOTS - 1 - i, first)
    return first, last


def kernel(left_hbm, pat_hbm, right_hbm, rpat_hbm, out, scale, own, pack, from_next, from_prev, from_far, pat, rpat, pats, raw, root, spare,
           left, right, mine, other, pair, chips, part, column, psend, precv, xsend, xrecv, rootsend, sparerecv, ownrecv, treesend,
           ysend, yrecv, csend, crecv, asend, arecv, zsend, zrecv, load, known):
    r, x = lax.axis_index("row"), lax.axis_index("col")
    z, g = r // NG, r % NG
    y, c = g // 2, g % 2

    def at_x(d):
        return (r, (x + d) % NX)

    def at_z(d):
        return (((z + d + NZ) % NZ) * NG + g, x)

    def at_y(d):
        return (z * NG + ((y + d) % NY) * 2 + c, x)

    sibling = (z * NG + y * 2 + 1 - c, x)

    def copy(src, dst, send, recv, to):
        return pltpu.make_async_remote_copy(src_ref=src, dst_ref=dst, send_sem=send, recv_sem=recv, device_id=to, device_id_type=MESH)

    barrier = pltpu.get_barrier_semaphore()
    peers = [at_x(d) for d in range(1, NX)] + [at_y(d) for d in range(1, NY)] + [sibling] + [at_z(d) for d in (1, NZ - 1)]
    for peer in peers:
        pl.semaphore_signal(barrier, inc=1, device_id=peer, device_id_type=MESH)

    loads = [pltpu.make_async_copy(left_hbm.at[s], own[s], load.at[s]) for s in range(S)]
    load_pattern = pltpu.make_async_copy(pat_hbm, pat, load.at[S + 1])
    load_pattern.start()
    for cp in loads:
        cp.start()
    is_root = jnp.logical_and(r % STEP == 0, r // STEP < S)
    load_right = pltpu.make_async_copy(right_hbm.at[pl.ds(0, NX * TILE)], raw, load.at[S])

    def piece_of(s, p, h):
        return right.at[pl.ds(pl.multiple_of(s * INNER + p * PIECE + h * PART, PART), PART)]

    @pl.when(is_root)
    def _():
        load_right_pattern = pltpu.make_async_copy(rpat_hbm, rpat, load.at[S + 2])
        load_right.start()
        load_right_pattern.start()
        load_right_pattern.wait()
        load_right.wait()
        for q, d in enumerate(ORDER):
            k = (x + d) % NX
            for j in range(COLS // TILE):
                tile = raw[pl.ds(pl.multiple_of(k * TILE, TILE), TILE), pl.ds(j * TILE, TILE)]
                root[pl.ds(q * TILE, TILE), pl.ds(j * TILE, TILE)] = jnp.where(rpat[j, k] != 0, tile, jnp.zeros_like(tile))

    load_pattern.wait()
    own_pattern = [[pat[s, 0, i] for i in range(TR)] for s in range(S)]
    for s in range(S):
        first, last = free_slots(own_pattern[s])
        loads[s].wait()
        for t in range(SLOTS):
            at = jnp.where(jnp.logical_and(own_pattern[s][TR - 2] != 0, first == t), TR - 2, t)
            at = jnp.where(jnp.logical_and(own_pattern[s][TR - 1] != 0, last == t), TR - 1, at)
            pack[s, t] = own[s][at]

    pl.semaphore_wait(barrier, len(peers))

    def wider(step):
        for to in (1 << step, NZ - (1 << step)):
            pl.semaphore_signal(known.at[step], inc=1, device_id=at_z(to), device_id_type=MESH)

    wider(0)

    my_panel = r // STEP

    def of_root(p, h):
        return root.at[pl.ds(pl.multiple_of(p * PIECE + h * PART, PART), PART)]

    spares = [spare.at[pl.ds(h * PART, PART)] for h in range(PARTS)]
    root_copies = []
    for h in range(PARTS):
        for d in (2, 1, 3):
            p = (g + 2 * d) % NG
            root_copies.append(copy(of_root((p + 1) % NG, h), spares[h], rootsend.at[2 * d - 1, h], sparerecv.at[h], at_y(d)))
            root_copies.append(copy(of_root(p, h), piece_of(my_panel, p, h), rootsend.at[2 * d - 2, h], ownrecv.at[my_panel, h], at_y(d)))
        p = g + 1 - 2 * c
        root_copies.append(copy(of_root(p, h), piece_of(my_panel, p, h), rootsend.at[6, h], ownrecv.at[my_panel, h], sibling))

    @pl.when(is_root)
    def _():
        for cp in root_copies:
            cp.start()
        start = pl.multiple_of(my_panel * INNER + g * PIECE, PIECE)
        right[pl.ds(start, PIECE)] = root[pl.ds(pl.multiple_of(g * PIECE, PIECE), PIECE)]

    pattern_copies = [copy(pat, pats[d], psend.at[d], precv.at[d], at_x(NX - d)) for d in range(1, NX)]
    for cp in pattern_copies:
        cp.start()
    halves = [pl.ds(0, HALF), pl.ds(HALF, HALF)]
    to_next = [[copy(pack.at[s, halves[h]], from_prev[s].at[halves[h]], xsend.at[0, s, h], xrecv.at[0, s, h], at_x(1)) for h in range(2)] for s in range(S)]
    to_prev = [[copy(pack.at[s, halves[h]], from_next[s].at[halves[h]], xsend.at[1, s, h], xrecv.at[1, s, h], at_x(NX - 1)) for h in range(2)] for s in range(S)]
    for s, h in ((0, 0), (1, 0), (2, 0), (0, 1)):
        to_next[s][h].start()
        to_prev[s][1 - h].start()
    far_next = [copy(from_prev[s].at[halves[0]], from_far[s].at[halves[0]], xsend.at[2, s, 0], xrecv.at[2, s, 0], at_x(1)) for s in range(S)]
    far_prev = [copy(from_next[s].at[halves[1]], from_far[s].at[halves[1]], xsend.at[2, s, 1], xrecv.at[2, s, 1], at_x(NX - 1)) for s in range(S)]

    def along_z(s, i, d):
        return [copy(piece_of(s, g, h), piece_of(s, g, h), treesend.at[i, h], ownrecv.at[s, h], at_z(d)) for h in range(PARTS)]

    def from_spare(s):
        p = g + 1 - 2 * c
        return [copy(spares[h], piece_of(s, p, h), rootsend.at[6, h], ownrecv.at[s, h], sibling) for h in range(PARTS)]

    zero = [STEP * s // NG for s in range(S)]
    for s in range(S):
        for h in range(PARTS):

            @pl.when(jnp.logical_and(z == zero[s], jnp.logical_and(g != STEP * s % NG, c == 0)))
            def _():
                copy(spares[h], spares[h], rootsend.at[6, h], sparerecv.at[h], sibling).wait_recv()
                from_spare(s)[h].start()

            @pl.when(jnp.logical_and(z == zero[s], g != STEP * s % NG))
            def _():
                along_z(s, 0, 1)[h].wait_recv()

            @pl.when(z == zero[s])
            def _():
                for i, d in enumerate((1, -1)):
                    along_z(s, i, d)[h].start()

    pl.semaphore_wait(known.at[0], 2)
    wider(1)
    pl.semaphore_wait(known.at[1], 2)
    wider(2)
    for s in range(S):

        @pl.when(z == zero[s])
        def _():
            for h in range(PARTS):
                for i, d in enumerate((4, -4)):
                    along_z(s, 2 + i, d)[h].start()
            for h in range(PARTS):
                for i, d in enumerate((2, -2)):
                    along_z(s, 4 + i, d)[h].start()

    for s in range(S):
        to_next[s][0].wait_recv()
        far_next[s].start()
        to_prev[s][1].wait_recv()
        far_prev[s].start()
        if s + 1 < S:
            to_next[s + 1][1].start()
            to_prev[s + 1][0].start()

    def place(s, q, pattern, tiles, low, high):
        for i, tile in zip((0, 1, 2, 3, 4, 5, 6, 7), (0, 1, 2, 3, 4, 5, low, high)):
            value = tiles[tile]
            left[pl.ds(i * TILE, TILE), pl.ds(base(s, q), TILE)] = jnp.where(pattern[i] != 0, value, jnp.zeros_like(value))

    for s in range(S):
        place(s, 0, own_pattern[s], own[s], TR - 2, TR - 1)

    rels = [(z - zero[s] + NZ) % NZ for s in range(S)]
    near = [jnp.where(rel % 8 == 4, -1, jnp.minimum(rel, NZ - rel)) for rel in rels]
    closest = jnp.where(jnp.logical_and(near[0] <= near[1], near[0] <= near[2]), 0, jnp.where(near[1] <= near[2], 1, 2))
    farthest = jnp.where(jnp.logical_and(near[2] >= near[0], near[2] >= near[1]), 2, jnp.where(near[1] >= near[0], 1, 0))
    panels = (closest, 3 - closest - farthest, farthest)
    y_copies, c_copies = [], []
    for n, s in enumerate(panels):
        rel = (z - STEP * s // NG + NZ) % NZ
        way = 1 - rel // 8 * 2
        relay_copies = [along_z(s, i, way * d) for i, d in enumerate((4, 3, 2, 1, -1))]
        sources = [(g + NG - 2 * d) % NG for d in range(NY)]
        y_copies.append([[copy(piece_of(s, g, h), piece_of(s, g, h), ysend.at[s, d - 1, h], yrecv.at[s, d - 1, h], at_y(d)) for d in range(1, NY)] for h in range(PARTS)])
        c_copies.append([[copy(piece_of(s, p, h), piece_of(s, p, h), csend.at[s, d, h], crecv.at[s, d, h], sibling) for d, p in enumerate(sources)] for h in range(PARTS)])
        for h in range(PARTS):

            @pl.when(rel != 0)
            def _():
                along_z(s, 0, 1)[h].wait_recv()

            @pl.when(rel == 4 + 8 * c)
            def _():
                relay_copies[0][h].start()

            @pl.when(rel % 8 == 4)
            def _():
                for cp in relay_copies[1:]:
                    cp[h].start()

            for d in (2, 1, 3):
                y_copies[n][h][d - 1].start()
            c_copies[n][h][0].start()

    for cp in pattern_copies:
        cp.wait_recv()

    def received(s, q, tiles):
        pattern = [pats[ORDER[q]][s, 0, i] for i in range(TR)]
        first, last = free_slots(pattern)
        place(s, q, pattern, tiles, first, last)

    for s in range(S):
        to_next[s][1].wait_recv()
        to_prev[s][0].wait_recv()
        received(s, 1, from_next[s])
        received(s, 2, from_prev[s])

    def to_sibling(n):
        for h in range(PARTS):
            for d in (1, 3, 2):
                y_copies[n][h][d - 1].wait_recv()
                c_copies[n][h][d].start()

    to_sibling(0)
    to_sibling(1)
    for s in range(S):
        far_next[s].wait_recv()
        far_prev[s].wait_recv()
        received(s, 3, from_far[s])
    pl.semaphore_wait(known.at[2], 2)
    to_sibling(2)

    for n, s in enumerate(panels):
        for h in range(PARTS):
            for d in range(NY):
                c_copies[n][h][d].wait_recv()
        inner = pl.ds(pl.multiple_of(s * INNER, INNER), INNER)
        for b in range(2):
            cols = pl.ds(b * 256, 256)
            total = jnp.dot(left[:, inner], right[inner, cols], preferred_element_type=jnp.float32)
            if n > 0:
                total = total + out[:, cols]
            if n == S - 1:
                total = total * total
                mine[:, cols] = jnp.sum(total, axis=0, keepdims=True)
            out[:, cols] = total

    across = copy(mine, other, asend.at[0], arecv.at[0], sibling)
    across.start()
    across.wait_recv()
    pair[...] = mine[...] + other[...]
    a_copies = [copy(pair, chips.at[d - 1], asend.at[d], arecv.at[d], at_y(d)) for d in range(1, NY)]
    for cp in a_copies:
        cp.start()
    for cp in a_copies:
        cp.wait_recv()
    part[...] = pair[...] + jnp.sum(chips[...], axis=0)
    z_copies = [copy(part, column.at[d - 1], zsend.at[d - 1], zrecv.at[d - 1], at_z(d)) for d in range(1, NZ)]
    for d in sorted(range(1, NZ), key=lambda d: -min(d, NZ - d)):
        z_copies[d - 1].start()
    for cp in z_copies:
        cp.wait_recv()
    rows_total = TR * TILE * NZ * NG
    scale[...] = rows_total / (part[...] + jnp.sum(column[...], axis=0))

    @pl.when(is_root)
    def _():
        for cp in root_copies:
            cp.wait_send()

    for s in range(S):
        rel = rels[s]
        for h in range(PARTS):

            @pl.when(rel == 0)
            def _():
                for i in range(6):
                    along_z(s, i, 1)[h].wait_send()

            @pl.when(jnp.logical_and(rel == 0, jnp.logical_and(g != STEP * s % NG, c == 0)))
            def _():
                from_spare(s)[h].wait_send()

            @pl.when(rel == 4 + 8 * c)
            def _():
                along_z(s, 0, 1)[h].wait_send()

            @pl.when(rel % 8 == 4)
            def _():
                for i in range(1, 5):
                    along_z(s, i, 1)[h].wait_send()

    flat = pattern_copies + far_next + far_prev + [across] + a_copies + z_copies
    for group_of in to_next + to_prev:
        flat = flat + group_of
    for panel in y_copies + c_copies:
        for group_of in panel:
            flat = flat + group_of
    for cp in flat:
        cp.wait_send()


def on_device(left_values, left_pattern, right_values, right_pattern):
    tiles = left_values.reshape(S, TR, TILE, TILE)
    pattern = left_pattern.transpose(0, 2, 1)
    rows = TR * TILE
    dma = pltpu.SemaphoreType.DMA
    box = lambda n: tuple(pltpu.VMEM((n, TILE, TILE), jnp.bfloat16) for _ in range(S))
    hbm, vmem = (pl.BlockSpec(memory_space=m) for m in (pltpu.HBM, pltpu.VMEM))
    squares, scale = pl.pallas_call(
        kernel,
        out_shape=(pltpu.VMEM((rows, COLS), jnp.float32), pltpu.VMEM((1, COLS), jnp.float32)),
        in_specs=[hbm] * 4,
        out_specs=(vmem, vmem),
        scratch_shapes=[
            box(TR),
            pltpu.VMEM((S, SLOTS, TILE, TILE), jnp.bfloat16),
            box(SLOTS), box(SLOTS), box(SLOTS),
            pltpu.SMEM((S, 1, TR), jnp.int32),
            pltpu.SMEM((COLS // TILE, TR), jnp.int32),
            tuple(pltpu.SMEM((S, 1, TR), jnp.int32) for _ in range(NX)),
            pltpu.VMEM((NX * TILE, COLS), jnp.bfloat16),
            pltpu.VMEM((NX * TILE, COLS), jnp.bfloat16),
            pltpu.VMEM((PIECE, COLS), jnp.bfloat16),
            pltpu.VMEM((rows, S * NX * TILE), jnp.bfloat16),
            pltpu.VMEM((S * NX * TILE, COLS), jnp.bfloat16),
            pltpu.VMEM((1, COLS), jnp.float32),
            pltpu.VMEM((1, COLS), jnp.float32),
            pltpu.VMEM((1, COLS), jnp.float32),
            pltpu.VMEM((NY - 1, 1, COLS), jnp.float32),
            pltpu.VMEM((1, COLS), jnp.float32),
            pltpu.VMEM((NZ - 1, 1, COLS), jnp.float32),
            dma((NX,)), dma((NX,)),
            dma((3, S, 2)), dma((3, S, 2)),
            dma((NG - 1, PARTS)), dma((PARTS,)), dma((S, PARTS)), dma((6, PARTS)),
            dma((S, NY - 1, PARTS)), dma((S, NY - 1, PARTS)),
            dma((S, NY, PARTS)), dma((S, NY, PARTS)),
            dma((NY,)), dma((NY,)),
            dma((NZ - 1,)), dma((NZ - 1,)),
            dma((S + 3,)),
            pltpu.SemaphoreType.REGULAR((3,)),
        ],
        compiler_params=pltpu.CompilerParams(collective_id=0, has_side_effects=True, vmem_limit_bytes=56 * 1024 * 1024),
    )(*[pltpu.with_memory_space_constraint(a, pltpu.HBM) for a in (tiles, pattern, right_values, right_pattern.T)])
    return squares * scale


def solution(mesh):
    in_specs = (P(None, "row", "col"), P(None, "row", "col"), P("row", "col"), P("row", "col"))
    out_specs = P("row", "col")
    return jax.shard_map(
        on_device, mesh=mesh, in_specs=in_specs, out_specs=out_specs, check_vma=False
    )
```

time: 54.4 us -> 52.3 us (0.961)
  the two profiles are of different devices: /device:TPU:2 before, /device:TPU:1 now
where the time goes in v3:
time: 52.3 us; the launch traced here: 52.2 us
  Pallas kernels  50.6 us (97%)
  other arithmetic  1.57 us (3%)
    pallas_call x1, Pallas kernels, on_device(): pl.pallas_call(kernel, out_shape=(pltpu.VMEM((rows, COLS), jnp.float32),...  50.6 us
    mul x1, other arithmetic, on_device(): return squares * scale  1.57 us

profile of v3, /device:TPU:1, one launch (start us, length us, event | category | flops | bytes accessed | tf_op | source)
XLA Modules:
  0.0 52.2 jit_solution(11772597121360528470)
XLA Ops:
  0.0 50.6 %shard_map.46 = (f32[1024,512]{1,0:T(8,128)S(1)}, f32[1,512]{1,0:T(1,128)S(1)}) custom-call(bf16[3,8,128,128]{3,2,1,0:T(8,128)(2,1)} %bitcast.5, s32[3,1,8]{2,1,0:T(1,128)} %bitcast.7, bf16[1024,512]{1,0:T(8,128)(2,1)} %right_hbm.1, s32[4,8]{1,0:T(4,128)} %bitcast.6), custom_call_target="tpu_custom_call" | custom-call | tf_op jit(solution)/shard_map/pallas_call | solution.py:334
  50.6 1.6 %broadcast_multiply_fusion = f32[1024,512]{1,0:T(8,128)} fusion(f32[1024,512]{1,0:T(8,128)S(1)} %get-tuple-element.7, f32[512]{0:T(512)S(1)} %bitcast.4), kind=kLoop, calls=%fused_computation | loop fusion | flops 524288 | bytes 4196352 | tf_op jit(solution)/shard_map/mul | solution.py:369

commit v4 on v3

--- a/solution.py
+++ b/solution.py
@@ -172,9 +172,6 @@
             for h in range(PARTS):
                 for i, d in enumerate((4, -4)):
                     along_z(s, 2 + i, d)[h].start()
-            for h in range(PARTS):
-                for i, d in enumerate((2, -2)):
-                    along_z(s, 4 + i, d)[h].start()
 
     for s in range(S):
         to_next[s][0].wait_recv()
@@ -224,6 +221,12 @@
             for d in (2, 1, 3):
                 y_copies[n][h][d - 1].start()
             c_copies[n][h][0].start()
+
+        @pl.when(rel == 0)
+        def _():
+            for i, d in enumerate((2, -2)):
+                for cp in along_z(s, 4 + i, d):
+                    cp.start()
 
     for cp in pattern_copies:
         cp.wait_recv()

time: 52.3 us -> 51.8 us (level)
  no operation moved by 1% of the time
where the time goes in v4:
time: 51.8 us; the launch traced here: 51.7 us
  Pallas kernels  50.1 us (97%)
  other arithmetic  1.57 us (3%)
    pallas_call x1, Pallas kernels, on_device(): pl.pallas_call(kernel, out_shape=(pltpu.VMEM((rows, COLS), jnp.float32),...  50.1 us
    mul x1, other arithmetic, on_device(): return squares * scale  1.57 us

profile of v4, /device:TPU:1, one launch (start us, length us, event | category | flops | bytes accessed | tf_op | source)
XLA Modules:
  0.0 51.7 jit_solution(11117193430911632065)
XLA Ops:
  0.0 50.1 %shard_map.46 = (f32[1024,512]{1,0:T(8,128)S(1)}, f32[1,512]{1,0:T(1,128)S(1)}) custom-call(bf16[3,8,128,128]{3,2,1,0:T(8,128)(2,1)} %bitcast.5, s32[3,1,8]{2,1,0:T(1,128)} %bitcast.7, bf16[1024,512]{1,0:T(8,128)(2,1)} %right_hbm.1, s32[4,8]{1,0:T(4,128)} %bitcast.6), custom_call_target="tpu_custom_call" | custom-call | tf_op jit(solution)/shard_map/pallas_call | solution.py:337
  50.1 1.6 %broadcast_multiply_fusion = f32[1024,512]{1,0:T(8,128)} fusion(f32[1024,512]{1,0:T(8,128)S(1)} %get-tuple-element.7, f32[512]{0:T(512)S(1)} %bitcast.4), kind=kLoop, calls=%fused_computation | loop fusion | flops 524288 | bytes 4196352 | tf_op jit(solution)/shard_map/mul | solution.py:372
